TPU v7x, 32 devices: a whole 2x2x4 slice. The times are simulated.
32 devices in a mesh: grp: 1, dap: 16 (over z, y, x), sub: 2 (over core).
Axes of the slice: x: 2, y: 2, z: 4, core: 2. Of those that a mesh axis runs over, the one named last changes fastest.
Arguments:
- pair_state: bfloat16 [384, 384, 128], P(('grp', 'dap', 'sub')), may hold values from -6 to 6
- residue_mask: int32 [384], P('grp'), may hold values 0 or 1
- norm_gain: float32 [2, 128], replicated, may hold values from 0.5 to 1.5
- edge_weight: bfloat16 [2, 128, 512], replicated, may hold values from -0.5 to 0.5
- gate_weight: bfloat16 [2, 128, 128], replicated, may hold values from -0.5 to 0.5
- out_weight: bfloat16 [2, 128, 128], replicated, may hold values from -0.5 to 0.5
- mix_gain: float32 [2, 128], replicated, may hold values from 0.5 to 1.5
Outputs:
- updated: bfloat16 [384, 384, 128], P(('grp', 'dap', 'sub'))
All inputs are finite; a program needn't handle non-finite values.
Results may differ from a plain program's by a relative error of at most 0.0075.
Values may be sent and summed in bfloat16 or wider, within the bound.
A program may use at most 64 MiB of HBM per device.

v0:
```python
import jax
import jax.numpy as jnp
from jax import lax
from jax.sharding import PartitionSpec as P


def layer_norm(values, gain, axis):
    average = jnp.mean(values, axis=axis, keepdims=True)
    centered = values - average
    variance = jnp.mean(centered * centered, axis=axis, keepdims=True)
    return centered * lax.rsqrt(variance + 1e-05) * gain


def triangle(left_side, right_side, outgoing):
    left_cols, right_cols = (
        lax.all_to_all(left_side, ("dap", "sub"), split_axis=0, concat_axis=1, tiled=True),
        lax.all_to_all(right_side, ("dap", "sub"), split_axis=0, concat_axis=1, tiled=True),
    )
    if outgoing:
        product = jnp.einsum(
            "hik,hjk->hij", left_cols, right_cols, preferred_element_type=jnp.float32
        )
    else:
        product = jnp.einsum(
            "hki,hkj->hij", left_cols, right_cols, preferred_element_type=jnp.float32
        )
    return lax.all_to_all(
        product.astype(jnp.bfloat16), ("dap", "sub"), split_axis=1, concat_axis=0, tiled=True
    )


def on_device(pair_state, residue_mask, norm_gain, edge_weight, gate_weight, out_weight, mix_gain):
    row_count = pair_state.shape[0]
    hidden = out_weight.shape[1]
    offset = lax.axis_index(("dap", "sub")) * row_count
    mask_values = residue_mask.astype(jnp.float32)
    row_mask = lax.dynamic_slice_in_dim(mask_values, offset, row_count)
    pair_mask = row_mask[:, None] * mask_values[None, :]
    current = pair_state
    for layer_index in range(2):
        values = current.astype(jnp.float32)
        normed = layer_norm(values, norm_gain[layer_index], -1).astype(jnp.bfloat16)
        projected = jnp.einsum(
            "rnc,cf->frn", normed, edge_weight[layer_index], preferred_element_type=jnp.float32
        )
        left_side = (
            jax.nn.sigmoid(projected[hidden : 2 * hidden]) * projected[:hidden] * pair_mask
        ).astype(jnp.bfloat16)
        right_side = (
            jax.nn.sigmoid(projected[3 * hidden :]) * projected[2 * hidden : 3 * hidden] * pair_mask
        ).astype(jnp.bfloat16)
        gating = jax.nn.sigmoid(
            jnp.einsum(
                "rnc,cd->rnd", normed, gate_weight[layer_index], preferred_element_type=jnp.float32
            )
        )
        mixed = triangle(left_side, right_side, layer_index == 0)
        normed_mix = layer_norm(
            mixed.astype(jnp.float32), mix_gain[layer_index][:, None, None], 0
        ).astype(jnp.bfloat16)
        update = jnp.einsum(
            "hrn,hc->rnc", normed_mix, out_weight[layer_index], preferred_element_type=jnp.float32
        )
        current = (values + gating * update).astype(jnp.bfloat16)
    return current


def solution(mesh):
    placed = (P(("grp", "dap", "sub"), None, None), P("grp"), P(), P(), P(), P(), P())
    return jax.shard_map(
        on_device,
        mesh=mesh,
        in_specs=placed,
        out_specs=P(("grp", "dap", "sub"), None, None),
        check_vma=False,
    )
```

profile of v0, /device:TPU:0, one launch (start us, length us, event | category | flops | bytes accessed | tf_op | source)
XLA Modules:
  0.0 272.4 jit_solution(1814150760018403661)
XLA Ops:
  0.0 1.8 copy.79
  2.6 1.5 convolution_bitcast_fusion.1
  4.1 2.4 fusion.28
  6.5 2.1 copy.86
  8.6 7.3 %all-to-all-start.1 = ((bf16[128,12,384]{2,1,0:T(8,128)(2,1)}), bf16[128,12,384]{2,1,0:T(8,128)(2,1)S(1)}, u32[]{:S(2)}, u32[]{:S(2)}) async-start(bf16[128,12,384]{2,1,0:T(8,128)(2,1)} %copy.86), calls=%async_computation.1 | async-start | bytes 3145728 | tf_op jit(solution)/shard_map/all_to_all | solution.py:17
  15.9 3.0 %copy.83 = bf16[128,12,384]{2,1,0:T(8,128)(2,1)} copy(bf16[128,12,384]{0,2,1:T(8,128)(2,1)} %get-tuple-element.9) | data formatting | bytes 2359296 | tf_op jit(solution)/shard_map/convert_element_type | solution.py:48
  18.9 34.8 %all-to-all-done.1 = bf16[128,12,384]{2,1,0:T(8,128)(2,1)S(1)} async-done(((bf16[128,12,384]{2,1,0:T(8,128)(2,1)}), bf16[128,12,384]{2,1,0:T(8,128)(2,1)S(1)}, u32[]{:S(2)}, u32[]{:S(2)}) %all-to-all-start.1) | async-done | bytes 1179680 | tf_op jit(solution)/shard_map/all_to_all | solution.py:17
  53.7 3.9 %all-to-all-start = ((bf16[128,12,384]{2,1,0:T(8,128)(2,1)}), bf16[128,12,384]{2,1,0:T(8,128)(2,1)}, u32[]{:S(2)}, u32[]{:S(2)}) async-start(bf16[128,12,384]{2,1,0:T(8,128)(2,1)} %copy.83), calls=%async_computation | async-start | bytes 3145728 | tf_op jit(solution)/shard_map/all_to_all | solution.py:16
  57.6 1.5 copy.120
  59.0 36.3 %all-to-all-done = bf16[128,12,384]{2,1,0:T(8,128)(2,1)} async-done(((bf16[128,12,384]{2,1,0:T(8,128)(2,1)}), bf16[128,12,384]{2,1,0:T(8,128)(2,1)}, u32[]{:S(2)}, u32[]{:S(2)}) %all-to-all-start) | async-done | bytes 1179680 | tf_op jit(solution)/shard_map/all_to_all | solution.py:16
  95.3 1.9 copy.118
  98.1 1.9 copy.91
  100.1 4.0 %all-to-all-start.2 = ((bf16[4,384,384]{2,0,1:T(4,128)(2,1)}), bf16[4,384,384]{2,0,1:T(4,128)(2,1)S(1)}, u32[]{:S(2)}, u32[]{:S(2)}) async-start(bf16[4,384,384]{2,0,1:T(4,128)(2,1)} %copy.91), calls=%async_computation.2 | async-start | bytes 2359296 | tf_op jit(solution)/shard_map/all_to_all | solution.py:27
  104.2 2.0 fusion.51
  106.2 26.8 %all-to-all-done.2 = bf16[4,384,384]{2,0,1:T(4,128)(2,1)S(1)} async-done(((bf16[4,384,384]{2,0,1:T(4,128)(2,1)}), bf16[4,384,384]{2,0,1:T(4,128)(2,1)S(1)}, u32[]{:S(2)}, u32[]{:S(2)}) %all-to-all-start.2) | async-done | bytes 1179680 | tf_op jit(solution)/shard_map/all_to_all | solution.py:27
  135.9 2.7 convert_reduce_fusion
  139.6 1.5 convolution_bitcast_fusion
  141.1 1.5 fusion.18
  142.6 2.1 copy.97
  144.7 3.8 %all-to-all-start.3 = ((bf16[128,12,384]{2,1,0:T(8,128)(2,1)}), bf16[128,12,384]{2,1,0:T(8,128)(2,1)}, u32[]{:S(2)}, u32[]{:S(2)}) async-start(bf16[128,12,384]{2,1,0:T(8,128)(2,1)} %copy.97), calls=%async_computation.3 | async-start | bytes 3145728 | tf_op jit(solution)/shard_map/all_to_all | solution.py:16
  148.4 2.1 copy.100
  150.5 35.6 %all-to-all-done.3 = bf16[128,12,384]{2,1,0:T(8,128)(2,1)} async-done(((bf16[128,12,384]{2,1,0:T(8,128)(2,1)}), bf16[128,12,384]{2,1,0:T(8,128)(2,1)}, u32[]{:S(2)}, u32[]{:S(2)}) %all-to-all-start.3) | async-done | bytes 1179680 | tf_op jit(solution)/shard_map/all_to_all | solution.py:16
  186.2 3.9 %all-to-all-start.4 = ((bf16[128,12,384]{2,1,0:T(8,128)(2,1)}), bf16[128,12,384]{2,1,0:T(8,128)(2,1)}, u32[]{:S(2)}, u32[]{:S(2)}) async-start(bf16[128,12,384]{2,1,0:T(8,128)(2,1)} %copy.100), calls=%async_computation.4 | async-start | bytes 3145728 | tf_op jit(solution)/shard_map/all_to_all | solution.py:17
  190.1 1.9 copy.122
  191.9 35.9 %all-to-all-done.4 = bf16[128,12,384]{2,1,0:T(8,128)(2,1)} async-done(((bf16[128,12,384]{2,1,0:T(8,128)(2,1)}), bf16[128,12,384]{2,1,0:T(8,128)(2,1)}, u32[]{:S(2)}, u32[]{:S(2)}) %all-to-all-start.4) | async-done | bytes 1179680 | tf_op jit(solution)/shard_map/all_to_all | solution.py:17
  227.8 1.9 copy.124
  230.7 1.9 copy.105
  232.6 4.0 %all-to-all-start.5 = ((bf16[4,384,384]{2,0,1:T(4,128)(2,1)}), bf16[4,384,384]{2,0,1:T(4,128)(2,1)S(1)}, u32[]{:S(2)}, u32[]{:S(2)}) async-start(bf16[4,384,384]{2,0,1:T(4,128)(2,1)} %copy.105), calls=%async_computation.5 | async-start | bytes 2359296 | tf_op jit(solution)/shard_map/all_to_all | solution.py:27
  236.7 2.0 fusion.54
  238.7 26.7 %all-to-all-done.5 = bf16[4,384,384]{2,0,1:T(4,128)(2,1)S(1)} async-done(((bf16[4,384,384]{2,0,1:T(4,128)(2,1)}), bf16[4,384,384]{2,0,1:T(4,128)(2,1)S(1)}, u32[]{:S(2)}, u32[]{:S(2)}) %all-to-all-start.5) | async-done | bytes 1179680 | tf_op jit(solution)/shard_map/all_to_all | solution.py:27
  268.4 2.6 fusion.11
  271.0 1.4 copy.109
  (58 shorter events, 9.6 us)
Async XLA Ops:
  0.0 2.3 copy-start.12
  0.0 2.4 copy-start.11
  0.0 2.5 copy-start.3
  2.5 1.5 copy-start.5
  8.6 45.1 %all-to-all-start.1 = ((bf16[128,12,384]{2,1,0:T(8,128)(2,1)}), bf16[128,12,384]{2,1,0:T(8,128)(2,1)S(1)}, u32[]{:S(2)}, u32[]{:S(2)}) async-start(bf16[128,12,384]{2,1,0:T(8,128)(2,1)} %copy.86), calls=%async_computation.1 | async-start | bytes 3145728 | tf_op jit(solution)/shard_map/all_to_all | solution.py:17
  53.7 41.6 %all-to-all-start = ((bf16[128,12,384]{2,1,0:T(8,128)(2,1)}), bf16[128,12,384]{2,1,0:T(8,128)(2,1)}, u32[]{:S(2)}, u32[]{:S(2)}) async-start(bf16[128,12,384]{2,1,0:T(8,128)(2,1)} %copy.83), calls=%async_computation | async-start | bytes 3145728 | tf_op jit(solution)/shard_map/all_to_all | solution.py:16
  59.0 38.1 %copy-start = (bf16[32,4,12,384]{3,1,2,0:T(4,128)(2,1)S(1)}, bf16[32,4,12,384]{3,1,2,0:T(4,128)(2,1)}, u32[]{:S(2)}) copy-start(bf16[32,4,12,384]{3,1,2,0:T(4,128)(2,1)} %copy.120) | copy-start | bytes 3538948
  98.1 5.9 %copy-start.13 = (f32[2,128]{1,0:T(2,128)S(1)}, f32[2,128]{1,0:T(2,128)}, u32[]{:S(2)}) copy-start(f32[2,128]{1,0:T(2,128)} %param.13) | copy-start | bytes 3076
  98.1 6.0 %copy-start.9 = (bf16[2,128,128]{2,1,0:T(8,128)(2,1)S(1)}, bf16[2,128,128]{2,1,0:T(8,128)(2,1)}, u32[]{:S(2)}) copy-start(bf16[2,128,128]{2,1,0:T(8,128)(2,1)} %param.11) | copy-start | bytes 196612
  100.1 32.9 %all-to-all-start.2 = ((bf16[4,384,384]{2,0,1:T(4,128)(2,1)}), bf16[4,384,384]{2,0,1:T(4,128)(2,1)S(1)}, u32[]{:S(2)}, u32[]{:S(2)}) async-start(bf16[4,384,384]{2,0,1:T(4,128)(2,1)} %copy.91), calls=%async_computation.2 | async-start | bytes 2359296 | tf_op jit(solution)/shard_map/all_to_all | solution.py:27
  135.9 3.7 %copy-start.4 = (bf16[2,128,512]{2,1,0:T(8,128)(2,1)S(1)}, bf16[2,128,512]{2,1,0:T(8,128)(2,1)}, u32[]{:S(2)}) copy-start(bf16[2,128,512]{2,1,0:T(8,128)(2,1)} %param.10) | copy-start | bytes 786436
  138.6 0.6 copy-start.1
  139.0 0.6 copy-start.7
  139.6 1.5 copy-start.6
  144.7 41.5 %all-to-all-start.3 = ((bf16[128,12,384]{2,1,0:T(8,128)(2,1)}), bf16[128,12,384]{2,1,0:T(8,128)(2,1)}, u32[]{:S(2)}, u32[]{:S(2)}) async-start(bf16[128,12,384]{2,1,0:T(8,128)(2,1)} %copy.97), calls=%async_computation.3 | async-start | bytes 3145728 | tf_op jit(solution)/shard_map/all_to_all | solution.py:16
  186.2 41.6 %all-to-all-start.4 = ((bf16[128,12,384]{2,1,0:T(8,128)(2,1)}), bf16[128,12,384]{2,1,0:T(8,128)(2,1)}, u32[]{:S(2)}, u32[]{:S(2)}) async-start(bf16[128,12,384]{2,1,0:T(8,128)(2,1)} %copy.100), calls=%async_computation.4 | async-start | bytes 3145728 | tf_op jit(solution)/shard_map/all_to_all | solution.py:17
  230.6 6.1 %copy-start.2 = (f32[12,384]{1,0:T(8,128)S(1)}, f32[12,384]{1,0:T(8,128)}, u32[]{:S(2)}) copy-start(f32[12,384]{1,0:T(8,128)} %copy-done.1) | copy-start | bytes 55300
  230.6 6.1 %copy-start.8 = (f32[12,384]{1,0:T(8,128)S(1)}, f32[12,384]{1,0:T(8,128)}, u32[]{:S(2)}) copy-start(f32[12,384]{1,0:T(8,128)} %copy-done.7) | copy-start | bytes 55300
  230.7 6.1 %copy-start.10 = (bf16[2,128,128]{2,1,0:T(8,128)(2,1)S(1)}, bf16[2,128,128]{2,1,0:T(8,128)(2,1)}, u32[]{:S(2)}) copy-start(bf16[2,128,128]{2,1,0:T(8,128)(2,1)} %param.11) | copy-start | bytes 196612
  232.6 32.9 %all-to-all-start.5 = ((bf16[4,384,384]{2,0,1:T(4,128)(2,1)}), bf16[4,384,384]{2,0,1:T(4,128)(2,1)S(1)}, u32[]{:S(2)}, u32[]{:S(2)}) async-start(bf16[4,384,384]{2,0,1:T(4,128)(2,1)} %copy.105), calls=%async_computation.5 | async-start | bytes 2359296 | tf_op jit(solution)/shard_map/all_to_all | solution.py:27
where the time goes:
time: 273 us; the launch traced here: 272 us
  waiting for transfers between devices  196 us (72%)
  starting transfers between devices  26.8 us (10%)
  local copies, waits for them, and re-layouts  25.9 us (9%)
  matrix products  14.2 us (5%)
  other arithmetic  9.04 us (3%)
    all_to_all x2, waiting for transfers between devices, triangle(): lax.all_to_all(left_side, ('dap', 'sub'), split_axis=0, concat_axis=1, ti...  71.9 us
    all_to_all x2, waiting for transfers between devices, triangle(): lax.all_to_all(right_side, ('dap', 'sub'), split_axis=0, concat_axis=1, t...  70.6 us
    all_to_all x2, waiting for transfers between devices, triangle(): lax.all_to_all(product.astype(jnp.bfloat16), ('dap', 'sub'), split_axis=1...  53.5 us
    all_to_all x2, starting transfers between devices, triangle(): lax.all_to_all(right_side, ('dap', 'sub'), split_axis=0, concat_axis=1, t...  11.2 us
    all_to_all x2, starting transfers between devices, triangle(): lax.all_to_all(product.astype(jnp.bfloat16), ('dap', 'sub'), split_axis=1...  7.95 us
    all_to_all x2, starting transfers between devices, triangle(): lax.all_to_all(left_side, ('dap', 'sub'), split_axis=0, concat_axis=1, ti...  7.65 us
  transfers between devices with their start and end apart: 6, of which 6 were waited for; matrix products, arithmetic and copies ran while one was open for 5% of the time, Pallas kernels for 0%

commit v1 on v0

v1 whole, which is shorter than its diff:
```python
import functools

import jax
import jax.numpy as jnp
from jax import lax
from jax.experimental import pallas as pl
from jax.experimental.pallas import tpu as pltpu
from jax.sharding import PartitionSpec as P

PER = 8
GROUP = 4
CHUNKS = 2
LANES = 128
TILE = 16
F32 = jnp.float32
BF16 = jnp.bfloat16


def sigmoid(x):
    return 0.5 * jnp.tanh(0.5 * x) + 0.5


def kernel(
    n, n_sub,
    z_ref, mask_s, mask_v, ng_ref, ew_ref, gw_ref, ow_ref, mg_ref,
    out_ref,
    wt, normed, send_l, send_r, recv_l, recv_r, stage, lh, rh, mf, send_m, recv_m,
    ss_l, ss_r, ss_m, rs_l, rs_r, rs_m,
):
    rows, cols, _ = z_ref.shape
    hidden = ow_ref.shape[1]
    owners = hidden // PER
    splits = n // owners
    block = rows * PER
    pairs = rows // 2
    pairs_chunk = pairs // CHUNKS
    span = pairs_chunk * TILE
    width = mf.shape[0] * LANES
    part = owners * rows

    me = lax.axis_index("dap") * n_sub + lax.axis_index("sub")
    split = lax.div(me, owners)
    mine = lax.rem(me, owners)
    first = split * owners

    def device(p):
        return {"dap": lax.div(p, n_sub), "sub": lax.rem(p, n_sub)}

    def loop(lo, hi, body):
        lax.fori_loop(lo, hi, lambda i, c: (body(i), c)[1], 0)

    barrier = pltpu.get_barrier_semaphore()
    loop(1, n, lambda k: pl.semaphore_signal(
        barrier, inc=1, device_id=device(lax.rem(me + k, n)),
        device_id_type=pl.DeviceIdType.MESH))

    def remote(src, dst, ssem, rsem, p):
        return pltpu.make_async_remote_copy(
            src_ref=src, dst_ref=dst, send_sem=ssem, recv_sem=rsem,
            device_id=device(p), device_id_type=pl.DeviceIdType.MESH)

    def left_copy(c, q):
        at = pl.ds(c * span, span)
        return remote(send_l.at[q, at], recv_l.at[mine, at], ss_l.at[c, q], rs_l.at[c, mine], first + q)

    def left_from(c, q):
        at = pl.ds(c * span, span)
        return remote(send_l.at[q, at], recv_l.at[q, at], ss_l.at[c, q], rs_l.at[c, q], first + q)

    def right_copy(c, p):
        at = pl.ds(c * span, span)
        return remote(send_r.at[lax.rem(p, owners), at], recv_r.at[me, at], ss_r.at[c, p], rs_r.at[c, me], p)

    def right_from(c, p):
        at = pl.ds(c * span, span)
        return remote(send_r.at[lax.rem(p, owners), at], recv_r.at[p, at], ss_r.at[c, p], rs_r.at[c, p], p)

    def mix_copy(q, p):
        return remote(send_m.at[q], recv_m.at[me], ss_m.at[p], rs_m.at[me], p)

    def mix_from(q, p):
        return remote(send_m.at[q], recv_m.at[p], ss_m.at[p], rs_m.at[p], p)

    columns = mask_v[...].astype(F32)

    def start_chunk(t, c):
        at = pl.ds(c * span, span)
        recv_l[mine, at] = send_l[mine, at]
        recv_r[me, at] = send_r[mine, at]

        if t == 0:
            def far(k):
                @pl.when(lax.div(lax.rem(me + k, n), owners) != split)
                def _():
                    right_copy(c, lax.rem(me + k, n)).start()
            loop(1, n, far)

        def near(k):
            q = lax.rem(mine + k, owners)
            right_copy(c, first + q).start()
            left_copy(c, q).start()
        loop(1, owners, near)

    def project(t, u, values_pair):
        sides = []
        for i in range(2):
            r = 2 * u + i
            values = values_pair[i]
            mean = jnp.mean(values, axis=-1, keepdims=True)
            centered = values - mean
            var = jnp.mean(centered * centered, axis=-1, keepdims=True)
            nr = (centered * lax.rsqrt(var + 1e-05) * ng_ref[pl.ds(t, 1), :]).astype(BF16)
            normed[r] = nr
            proj = lax.dot_general(wt[...], nr, (((1,), (1,)), ((), ())), preferred_element_type=F32)
            mask = columns * mask_s[me * rows + r].astype(F32)
            sides.append((
                sigmoid(proj[hidden:2 * hidden]) * proj[:hidden] * mask,
                sigmoid(proj[3 * hidden:]) * proj[2 * hidden:3 * hidden] * mask,
            ))
        at = pl.ds(pl.multiple_of(u * TILE, TILE), TILE)
        for ref, k in ((send_l, 0), (send_r, 1)):
            both = jnp.concatenate(
                [sides[i][k].reshape(owners, PER, cols) for i in range(2)], axis=1)
            ref[:, at, :] = both.astype(BF16)

    def finish(t, u, z):
        at = pl.ds(pl.multiple_of(u * TILE, TILE), TILE)
        if t == 0:
            got = recv_m[pl.ds(first, owners), at, :].astype(F32)
        else:
            got = recv_m[pl.ds(0, owners), at, :].astype(F32)
            for s in range(1, splits):
                got = got + recv_m[pl.ds(s * owners, owners), at, :].astype(F32)
        result = []
        for i in range(2):
            r = 2 * u + i
            mixed = got[:, i * PER:(i + 1) * PER, :].reshape(hidden, cols)
            mean = jnp.mean(mixed, axis=0, keepdims=True)
            centered = mixed - mean
            var = jnp.mean(centered * centered, axis=0, keepdims=True)
            nm = (centered * lax.rsqrt(var + 1e-05) * mg_ref[t]).astype(BF16)
            update = lax.dot_general(nm, ow_ref[t], (((0,), (0,)), ((), ())), preferred_element_type=F32)
            gate = sigmoid(jnp.dot(normed[r], gw_ref[t], preferred_element_type=F32))
            new = (z[r].astype(F32) + gate * update).astype(BF16)
            out_ref[r] = new
            result.append(new.astype(F32))
        return result

    def sort(src, base, dst, at, g):
        for v in range(cols // LANES):
            lanes = pl.ds(v * LANES, LANES)
            stage[v] = src[pl.ds(base + g * GROUP, GROUP), :, lanes].astype(F32).reshape(stage.shape[1:])
            for h in range(PER):
                dst[h, pl.ds(pl.multiple_of(at + g * GROUP * rows, TILE), GROUP * rows), lanes] = stage[
                    v, pl.ds(h, GROUP * rows, stride=PER), :].astype(BF16)

    def spread(h, count, product):
        for v in range(width // LANES):
            mf[v, pl.ds(h, count, stride=PER), :] = product[:, v * LANES:(v + 1) * LANES]

    def gather(slot, q, jc):
        for v in range(width // LANES):
            send_m[slot, :, pl.ds(jc * width + v * LANES, LANES)] = mf[
                v, pl.ds(pl.multiple_of(q * block, TILE), block), :].astype(BF16)

    def wait_left(g):
        def one(q):
            @pl.when(q != mine)
            def _():
                for c in range(CHUNKS):
                    left_from(c, q).wait_recv()
        loop(g * GROUP, (g + 1) * GROUP, one)

    def wait_right(base, g):
        def one(p):
            @pl.when(p != me)
            def _():
                for c in range(CHUNKS):
                    right_from(c, p).wait_recv()
        loop(base + g * GROUP, base + (g + 1) * GROUP, one)

    def prepare(t):
        wt[...] = ew_ref[t].astype(F32).T.astype(BF16)

    def project_all(t):
        for c in range(CHUNKS):
            def body(u):
                if t == 0:
                    project(t, u, [z_ref[2 * u].astype(F32), z_ref[2 * u + 1].astype(F32)])
                else:
                    project(t, u, finish(0, u, z_ref))
            loop(c * pairs_chunk, (c + 1) * pairs_chunk, body)
            if t == 0 and c == 0:
                pl.semaphore_wait(barrier, n - 1)
            start_chunk(t, c)

    def wait_sent(t):
        def one(p):
            @pl.when(p != me)
            def _():
                for c in range(CHUNKS):
                    right_from(c, p).wait_send()
        if t == 0:
            loop(0, n, one)
        else:
            loop(first, first + owners, one)

        def two(q):
            @pl.when(q != mine)
            def _():
                for c in range(CHUNKS):
                    left_from(c, q).wait_send()
        loop(0, owners, two)

    prepare(0)
    project_all(0)
    prepare(1)

    def left_in(g):
        wait_left(g)
        sort(recv_l, 0, lh, 0, g)
    loop(0, owners // GROUP, left_in)

    for jc in range(cols // width):
        sources = width // rows

        def right_in(g):
            wait_right(jc * sources, g)
            sort(recv_r, jc * sources, rh, 0, g)
        loop(0, sources // GROUP, right_in)
        for h in range(PER):
            spread(h, part, lax.dot_general(
                lh[h], rh[h], (((1,), (1,)), ((), ())), preferred_element_type=F32))
        loop(0, owners, lambda q: gather(q, q, jc))

    recv_m[me] = send_m[mine]
    loop(1, owners, lambda k: mix_copy(
        lax.rem(mine + k, owners), first + lax.rem(mine + k, owners)).start())
    wait_sent(0)

    def mix_in(p):
        @pl.when(p != me)
        def _():
            mix_from(p - first, p).wait_recv()
    loop(first, first + owners, mix_in)

    project_all(1)

    def mix_out(p):
        @pl.when(p != me)
        def _():
            mix_from(p - first, p).wait_send()
    loop(first, first + owners, mix_out)

    def both_in(g):
        wait_left(g)
        sort(recv_l, 0, lh, 0, g)
        wait_right(first, g)
        sort(recv_r, first, rh, 0, g)
    loop(0, owners // GROUP, both_in)

    devices = width // rows
    for ic in range(cols // width):
        for jc in range(cols // width):
            for h in range(PER):
                spread(h, width, lax.dot_general(
                    lh[h, :, pl.ds(ic * width, width)],
                    rh[h, pl.ds(0, part), pl.ds(jc * width, width)],
                    (((0,), (0,)), ((), ())), preferred_element_type=F32))
            loop(0, devices, lambda q: gather(ic * devices + q, q, jc))

    recv_m[me] = send_m[me]

    def send_mix(k):
        p = lax.rem(me + k, n)
        mix_copy(p, p).start()
    loop(1, n, send_mix)
    wait_sent(1)

    def mix_in_all(k):
        p = lax.rem(me + k, n)
        mix_from(p, p).wait_recv()
    loop(1, n, mix_in_all)

    loop(0, pairs, lambda u: (finish(1, u, out_ref), None)[1])

    def mix_out_all(k):
        p = lax.rem(me + k, n)
        mix_from(p, p).wait_send()
    loop(1, n, mix_out_all)


def on_device(n, n_sub, pair_state, residue_mask, norm_gain, edge_weight, gate_weight, out_weight, mix_gain):
    rows, cols, chan = pair_state.shape
    hidden = out_weight.shape[1]
    owners = hidden // PER
    block = rows * PER
    width = min(cols, 32 * rows)
    vmem = pl.BlockSpec(memory_space=pltpu.VMEM)
    dma = pltpu.SemaphoreType.DMA
    flops = 2 * 2 * rows * cols * chan * (5 * hidden + chan) + 2 * 2 * PER * owners * rows * cols * cols
    return pl.pallas_call(
        functools.partial(kernel, n, n_sub),
        out_shape=jax.ShapeDtypeStruct(pair_state.shape, BF16),
        in_specs=[vmem, pl.BlockSpec(memory_space=pltpu.SMEM)] + [vmem] * 6,
        out_specs=vmem,
        scratch_shapes=[
            pltpu.VMEM((4 * hidden, chan), BF16),
            pltpu.VMEM((rows, cols, chan), BF16),
            pltpu.VMEM((owners, block, cols), BF16),
            pltpu.VMEM((owners, block, cols), BF16),
            pltpu.VMEM((owners, block, cols), BF16),
            pltpu.VMEM((n, block, cols), BF16),
            pltpu.VMEM((cols // LANES, GROUP * block, LANES), F32),
            pltpu.VMEM((PER, owners * rows, cols), BF16),
            pltpu.VMEM((PER, width, cols), BF16),
            pltpu.VMEM((width // LANES, PER * width, LANES), F32),
            pltpu.VMEM((n, block, cols), BF16),
            pltpu.VMEM((n, block, cols), BF16),
            dma((CHUNKS, owners)),
            dma((CHUNKS, n)),
            dma((n,)),
            dma((CHUNKS, owners)),
            dma((CHUNKS, n)),
            dma((n,)),
        ],
        compiler_params=pltpu.CompilerParams(
            collective_id=0, has_side_effects=True, vmem_limit_bytes=60 * 2**20),
        cost_estimate=pl.CostEstimate(
            flops=flops, bytes_accessed=4 * rows * cols * chan, transcendentals=0),
    )(
        pair_state, residue_mask, residue_mask.reshape(1, -1), norm_gain, edge_weight,
        gate_weight, out_weight, mix_gain[:, :, None],
    )


def solution(mesh):
    placed = (P(("grp", "dap", "sub"), None, None), P("grp"), P(), P(), P(), P(), P())
    n_sub = mesh.shape["sub"]
    return jax.shard_map(
        functools.partial(on_device, mesh.shape["dap"] * n_sub, n_sub),
        mesh=mesh,
        in_specs=placed,
        out_specs=P(("grp", "dap", "sub"), None, None),
        check_vma=False,
    )
```

time: 273 us -> 188 us (0.69)
  the two profiles are of different devices: /device:TPU:0 before, /device:TPU:31 now
where the time goes in v1:
time: 188 us; the launch traced here: 187 us
  Pallas kernels  182 us (97%)
  local copies, waits for them, and re-layouts  5.09 us (3%)
    pallas_call x1, Pallas kernels, on_device(): pl.pallas_call(functools.partial(kernel, n, n_sub), out_shape=jax.ShapeDt...  182 us

profile of v1, /device:TPU:31, one launch (start us, length us, event | category | flops | bytes accessed | tf_op | source)
XLA Modules:
  0.0 187.4 jit_solution(10867220173905037370)
XLA Ops:
  0.0 1.3 reshape.3.mask_v
  1.3 1.5 copy.8.mg_ref
  2.7 182.3 %shard_map.73 = bf16[12,384,128]{2,1,0:T(8,128)(2,1)} custom-call(bf16[12,384,128]{2,1,0:T(8,128)(2,1)} %z_ref.1, s32[384]{0:T(512)} %mask_s.1, s32[1,384]{1,0:T(1,128)} %reshape.3.mask_v, f32[2,128]{1,0:T(2,128)} %ng_ref.1, bf16[2,128,512]{2,1,0:T(8,128)(2,1)} %ew_ref.1, bf16[2,128,128]{2,1,0:T(8,128)(2,1)} %gw_ref.1, bf16[2,128,128]{2,1,0:T(8,128)(2,1)} %ow_ref.1, ...), custom_call_target="tpu_custom_call" | custom-call | flops 2717908992 | bytes 2359296 | tf_op jit(solution)/shard_map/pallas_call | solution.py:302
  185.1 2.4 %copy.10 = bf16[12,384,128]{2,1,0:T(8,128)(2,1)} copy(bf16[12,384,128]{2,1,0:T(8,128)(2,1)} %shard_map.73) | data formatting | bytes 2359296

commit v2 on v0

v2 whole, which is shorter than its diff:
```python
import functools

import jax
import jax.numpy as jnp
from jax import lax
from jax.experimental import pallas as pl
from jax.experimental.pallas import tpu as pltpu
from jax.sharding import PartitionSpec as P

PER = 8
GROUP = 4
LANES = 128
TILE = 16
F32 = jnp.float32
BF16 = jnp.bfloat16


def sigmoid(x):
    return 0.5 * jnp.tanh(0.5 * x) + 0.5


def kernel(
    n, n_sub,
    z_ref, mask_s, mask_v, ng_ref, ew_ref, gw_ref, ow_ref, mg_ref,
    out_ref,
    wt, gain, normed, send_l, send_r, recv_l, recv_r, stage, lh, rh, mf, send_m, recv_m,
    ss_l, ss_r, ss_m, rs_l, rs_r, rs_m,
):
    rows, cols, _ = z_ref.shape
    hidden = ow_ref.shape[1]
    owners = hidden // PER
    splits = n // owners
    block = rows * PER
    pairs = rows // 2
    part = owners * rows
    chunks = cols // LANES
    groups = owners // GROUP

    me = lax.axis_index("dap") * n_sub + lax.axis_index("sub")
    split = lax.div(me, owners)
    mine = lax.rem(me, owners)
    first = split * owners

    def device(p):
        return {"dap": lax.div(p, n_sub), "sub": lax.rem(p, n_sub)}

    def loop(lo, hi, body):
        lax.fori_loop(lo, hi, lambda i, c: (body(i), c)[1], 0)

    def turn(s, count):
        return jnp.where(2 * split >= splits, count - 1 - s, s)

    def lanes(v):
        return pl.ds(pl.multiple_of(v * LANES, LANES), LANES)

    barrier = pltpu.get_barrier_semaphore()
    loop(1, n, lambda k: pl.semaphore_signal(
        barrier, inc=1, device_id=device(lax.rem(me + k, n)),
        device_id_type=pl.DeviceIdType.MESH))

    def remote(src, dst, ssem, rsem, p):
        return pltpu.make_async_remote_copy(
            src_ref=src, dst_ref=dst, send_sem=ssem, recv_sem=rsem,
            device_id=device(p), device_id_type=pl.DeviceIdType.MESH)

    def left_copy(v, q, slot):
        return remote(send_l.at[q, v], recv_l.at[slot, v], ss_l.at[v, q], rs_l.at[v, slot], first + q)

    def right_copy(v, p, slot):
        return remote(
            send_r.at[lax.rem(p, owners), v], recv_r.at[slot, v], ss_r.at[v, p], rs_r.at[v, slot], p)

    def mix_copy(v, q, p, slot):
        return remote(send_m.at[q, v], recv_m.at[slot, v], ss_m.at[v, p], rs_m.at[v, slot], p)

    def away(k, s):
        return lax.rem(first + s * owners, n) + lax.rem(mine + k, owners)

    def start_left(v):
        recv_l[mine, v] = send_l[mine, v]
        loop(1, owners, lambda k: left_copy(v, lax.rem(mine + k, owners), mine).start())

    def start_right(v):
        recv_r[me, v] = send_r[mine, v]
        loop(1, owners, lambda k: right_copy(v, away(k, 0), me).start())

    def start_all(v, last):
        recv_l[mine, v] = send_l[mine, v]
        recv_r[me, v] = send_r[mine, v]

        def far(k):
            for s in range(1, splits):
                right_copy(v, away(k, s), me).start()

        def near(k):
            if not last:
                far(k)
            right_copy(v, away(k, 0), me).start()
            left_copy(v, lax.rem(mine + k, owners), mine).start()
        loop(1, owners, near)
        if last:
            loop(0, owners, far)
        else:
            far(0)

    def project(t, u, v, values):
        mean = jnp.mean(values, axis=-1, keepdims=True)
        centered = values - mean
        var = jnp.mean(centered * centered, axis=-1, keepdims=True)
        nr = (centered * lax.rsqrt(var + 1e-05) * ng_ref[pl.ds(t, 1), :]).astype(BF16)
        normed[pl.ds(2 * u, 2), lanes(v), :] = nr.reshape(2, LANES, -1)
        proj = lax.dot_general(wt[...], nr, (((1,), (1,)), ((), ())), preferred_element_type=F32)
        columns = mask_v[:, lanes(v)].astype(F32)
        mask = jnp.concatenate(
            [columns * mask_s[me * rows + 2 * u + i].astype(F32) for i in range(2)], axis=1)
        at = pl.ds(pl.multiple_of(u * TILE, TILE), TILE)
        for ref, k in ((send_l, 0), (send_r, 2)):
            side = sigmoid(proj[(k + 1) * hidden:(k + 2) * hidden]) * proj[k * hidden:(k + 1) * hidden] * mask
            both = jnp.concatenate(
                [side[:, i * LANES:(i + 1) * LANES].reshape(owners, PER, LANES) for i in range(2)], axis=1)
            ref[:, v, at, :] = both.astype(BF16)

    def finish(t, u, v, z):
        at = pl.ds(pl.multiple_of(u * TILE, TILE), TILE)
        if t == 0:
            got = recv_m[pl.ds(first, owners), v, at, :].astype(F32)
        else:
            got = recv_m[pl.ds(0, owners), v, at, :].astype(F32)
            for s in range(1, splits):
                got = got + recv_m[pl.ds(s * owners, owners), v, at, :].astype(F32)
        mixed = jnp.concatenate(
            [got[:, i * PER:(i + 1) * PER, :].reshape(hidden, LANES) for i in range(2)], axis=1)
        mean = jnp.mean(mixed, axis=0, keepdims=True)
        centered = mixed - mean
        var = jnp.mean(centered * centered, axis=0, keepdims=True)
        nm = (centered * lax.rsqrt(var + 1e-05) * gain[...]).astype(BF16)
        update = lax.dot_general(nm, ow_ref[t], (((0,), (0,)), ((), ())), preferred_element_type=F32)
        two = (pl.ds(2 * u, 2), lanes(v))
        gate = sigmoid(jnp.dot(
            normed[two[0], two[1], :].reshape(update.shape), gw_ref[t], preferred_element_type=F32))
        old = z[two[0], two[1], :].astype(F32).reshape(update.shape)
        new = (old + gate * update).astype(BF16)
        out_ref[two[0], two[1], :] = new.reshape(2, LANES, -1)
        return new.astype(F32)

    def sort(src, base, dst, g, v):
        stage[...] = src[pl.ds(base + g * GROUP, GROUP), v].astype(F32).reshape(stage.shape)
        for h in range(PER):
            dst[h, pl.ds(pl.multiple_of(g * GROUP * rows, TILE), GROUP * rows), lanes(v)] = stage[
                pl.ds(h, GROUP * rows, stride=PER), :].astype(BF16)

    def wait_left(g, v):
        def one(q):
            @pl.when(q != mine)
            def _():
                left_copy(v, q, q).wait_recv()
        loop(g * GROUP, (g + 1) * GROUP, one)

    def wait_right(base, g, v):
        def one(p):
            @pl.when(p != me)
            def _():
                right_copy(v, p, p).wait_recv()
        loop(base + g * GROUP, base + (g + 1) * GROUP, one)

    def prepare(t):
        wt[...] = ew_ref[t].astype(F32).T.astype(BF16)

    def prepare_gain(t):
        gain[...] = jnp.broadcast_to(mg_ref[pl.ds(t, 1), :], (hidden, hidden)).T[:, :1]

    def wait_sent(t):
        def one(k):
            for v in range(chunks):
                if t == 0:
                    for s in range(1, splits):
                        right_copy(v, away(k, s), me).wait_send()

                @pl.when(k > 0)
                def _():
                    right_copy(v, away(k, 0), me).wait_send()
                    left_copy(v, lax.rem(mine + k, owners), mine).wait_send()
        loop(0, owners, one)

    prepare(0)
    prepare_gain(0)
    for v in range(chunks):
        loop(0, pairs, lambda u: project(
            0, u, v, z_ref[pl.ds(2 * u, 2), lanes(v), :].astype(F32).reshape(2 * LANES, -1)))
        if v == 0:
            pl.semaphore_wait(barrier, n - 1)
        start_all(v, v == chunks - 1)
    prepare(1)

    def left_in(g):
        for v in range(chunks):
            wait_left(g, v)
            sort(recv_l, 0, lh, g, v)
    loop(0, groups, left_in)

    def right_in(i):
        g = turn(i, n // GROUP)
        for v in range(chunks):
            wait_right(0, g, v)
            sort(recv_r, 0, rh, g, v)

    done, sorted_by = 0, None
    for s in range(chunks):
        need = -(-(s + 1) * LANES // (GROUP * rows))
        if sorted_by is None and need >= (splits + 1) // 2 * groups:
            sorted_by = s
        loop(done, need, right_in)
        done = need
        v = turn(s, chunks)
        for h in range(PER):
            mf[pl.ds(h, part, stride=PER), :] = lax.dot_general(
                lh[h], rh[h, lanes(v), :], (((1,), (1,)), ((), ())), preferred_element_type=F32)

        def hand_back(k):
            q = lax.rem(mine + k, owners)
            send_m[q, v] = mf[pl.ds(pl.multiple_of(q * block, TILE), block), :].astype(BF16)

            @pl.when(k > 0)
            def _():
                mix_copy(v, q, first + q, me).start()
        loop(0, owners, hand_back)
        recv_m[me, v] = send_m[mine, v]
    wait_sent(0)

    for s in range(chunks):
        v = turn(s, chunks)

        def mix_in(k):
            p = away(k, 0)
            mix_copy(v, p - first, p, p).wait_recv()
        loop(1, owners, mix_in)
        loop(0, pairs, lambda u: project(1, u, v, finish(0, u, v, z_ref)))
        start_left(v)
        if s == sorted_by:
            start_right(turn(0, chunks))
    for s in range(1, chunks):
        start_right(turn(s, chunks))
    prepare_gain(1)

    def mix_out(k):
        for v in range(chunks):
            mix_copy(v, lax.rem(mine + k, owners), away(k, 0), me).wait_send()
    loop(1, owners, mix_out)

    for s in range(chunks):
        v = turn(s, chunks)

        def left_again(g):
            wait_left(g, v)
            sort(recv_l, 0, lh, g, v)
        loop(0, groups, left_again)
    for s in range(chunks):
        v = turn(s, chunks)

        def right_again(g):
            wait_right(first, g, v)
            sort(recv_r, first, rh, g, v)
        loop(0, groups, right_again)
        for h in range(PER):
            mf[pl.ds(h, cols, stride=PER), :] = lax.dot_general(
                lh[h], rh[h, pl.ds(0, part), lanes(v)], (((0,), (0,)), ((), ())),
                preferred_element_type=F32)

        def pack(p):
            send_m[p, v] = mf[pl.ds(pl.multiple_of(p * block, TILE), block), :].astype(BF16)

        def hand_out(k):
            for i in range(1, splits):
                p = away(k, i)
                pack(p)
                mix_copy(v, p, p, me).start()
            p = away(k, 0)
            pack(p)

            @pl.when(k > 0)
            def _():
                mix_copy(v, p, p, me).start()
        loop(0, owners, hand_out)
        recv_m[me, v] = send_m[me, v]
    wait_sent(1)

    for s in [chunks // 2] + [s for s in range(chunks) if s != chunks // 2]:
        v = turn(s, chunks)

        def mix_in_all(k):
            p = lax.rem(me + k, n)
            mix_copy(v, p, p, p).wait_recv()
        loop(1, n, mix_in_all)
        loop(0, pairs, lambda u: (finish(1, u, v, out_ref), None)[1])

    def mix_out_all(k):
        p = lax.rem(me + k, n)
        for v in range(chunks):
            mix_copy(v, p, p, me).wait_send()
    loop(1, n, mix_out_all)


def on_device(n, n_sub, pair_state, residue_mask, norm_gain, edge_weight, gate_weight, out_weight, mix_gain):
    rows, cols, chan = pair_state.shape
    hidden = out_weight.shape[1]
    owners = hidden // PER
    block = rows * PER
    chunks = cols // LANES
    vmem = pl.BlockSpec(memory_space=pltpu.VMEM)
    dma = pltpu.SemaphoreType.DMA
    flops = 2 * 2 * rows * cols * chan * (5 * hidden + chan) + 2 * 2 * PER * owners * rows * cols * cols
    return pl.pallas_call(
        functools.partial(kernel, n, n_sub),
        out_shape=jax.ShapeDtypeStruct(pair_state.shape, BF16),
        in_specs=[vmem, pl.BlockSpec(memory_space=pltpu.SMEM)] + [vmem] * 6,
        out_specs=vmem,
        scratch_shapes=[
            pltpu.VMEM((4 * hidden, chan), BF16),
            pltpu.VMEM((hidden, 1), F32),
            pltpu.VMEM((rows, cols, chan), BF16),
            pltpu.VMEM((owners, chunks, block, LANES), BF16),
            pltpu.VMEM((owners, chunks, block, LANES), BF16),
            pltpu.VMEM((owners, chunks, block, LANES), BF16),
            pltpu.VMEM((n, chunks, block, LANES), BF16),
            pltpu.VMEM((GROUP * block, LANES), F32),
            pltpu.VMEM((PER, owners * rows, cols), BF16),
            pltpu.VMEM((PER, n * rows, cols), BF16),
            pltpu.VMEM((PER * cols, LANES), F32),
            pltpu.VMEM((n, chunks, block, LANES), BF16),
            pltpu.VMEM((n, chunks, block, LANES), BF16),
            dma((chunks, owners)),
            dma((chunks, n)),
            dma((chunks, n)),
            dma((chunks, owners)),
            dma((chunks, n)),
            dma((chunks, n)),
        ],
        compiler_params=pltpu.CompilerParams(
            collective_id=0, has_side_effects=True, vmem_limit_bytes=60 * 2**20),
        cost_estimate=pl.CostEstimate(
            flops=flops, bytes_accessed=4 * rows * cols * chan, transcendentals=0),
    )(
        pair_state, residue_mask, residue_mask.reshape(1, -1), norm_gain, edge_weight,
        gate_weight, out_weight, mix_gain,
    )


def solution(mesh):
    placed = (P(("grp", "dap", "sub"), None, None), P("grp"), P(), P(), P(), P(), P())
    n_sub = mesh.shape["sub"]
    return jax.shard_map(
        functools.partial(on_device, mesh.shape["dap"] * n_sub, n_sub),
        mesh=mesh,
        in_specs=placed,
        out_specs=P(("grp", "dap", "sub"), None, None),
        check_vma=False,
    )
```

time: 273 us -> 163 us (0.60)
  waiting for transfers between devices: 196 us -> 0 us
  Pallas kernels: 0 us -> 159 us
  starting transfers between devices: 26.8 us -> 0 us
  local copies, waits for them, and re-layouts: 25.9 us -> 3.6 us
  matrix products: 14.2 us -> 0 us
  other arithmetic: 9.04 us -> 0 us
    all_to_all x6 -> x0, waiting for transfers between devices: 196 us -> none  [the longest x2 71.9 us: triangle(): lax.all_to_all(left_side, ('dap', 'sub'), split_axis=0, concat_axis=1, ti...]
    pallas_call x0 -> x1, Pallas kernels: none -> 159 us  [on_device(): pl.pallas_call(functools.partial(kernel, n, n_sub), out_shape=jax.ShapeDt...]
    all_to_all x6 -> x0, starting transfers between devices: 26.8 us -> none  [the longest x2 11.2 us: triangle(): lax.all_to_all(right_side, ('dap', 'sub'), split_axis=0, concat_axis=1, t...]
    convert_element_type x11 -> x0, local copies, waits for them, and re-layouts: 16.2 us -> none  [the longest x2 5.06 us: on_device(): left_side = (jax.nn.sigmoid(projected[hidden:2 * hidden]) * projected[:hi...]
    dot_general x8 -> x0, matrix products: 14.2 us -> none  [the longest x2 5.29 us: on_device(): jnp.einsum('hrn,hc->rnc', normed_mix, out_weight[layer_index], preferred_...]
    all_to_all x4 -> x0, local copies, waits for them, and re-layouts: 7.06 us -> none  [the longest x2 3.73 us: triangle(): lax.all_to_all(left_side, ('dap', 'sub'), split_axis=0, concat_axis=1, ti...]
    convert_element_type x5 -> x0, other arithmetic: 5.46 us -> none  [the longest x2 3.9 us: on_device(): left_side = (jax.nn.sigmoid(projected[hidden:2 * hidden]) * projected[:hi...]
    reduce_sum x7 -> x0, other arithmetic: 3.44 us -> none  [the longest x4 2.28 us: layer_norm(): variance = jnp.mean(centered * centered, axis=axis, keepdims=True)]
  transfers between devices with their start and end apart: 6 -> 0, of which waited for: 6 -> 0; matrix products, arithmetic and copies ran while one was open for 5% -> 0% of each run, Pallas kernels for 0% -> 0%
where the time goes in v2:
time: 163 us; the launch traced here: 162 us
  Pallas kernels  159 us (98%)
  local copies, waits for them, and re-layouts  3.6 us (2%)
    pallas_call x1, Pallas kernels, on_device(): pl.pallas_call(functools.partial(kernel, n, n_sub), out_shape=jax.ShapeDt...  159 us

profile of v2, /device:TPU:0, one launch (start us, length us, event | category | flops | bytes accessed | tf_op | source)
XLA Modules:
  0.0 162.4 jit_solution(2146679342639040138)
XLA Ops:
  0.0 1.2 reshape.3.mask_v
  1.2 158.8 %shard_map.73 = bf16[12,384,128]{2,1,0:T(8,128)(2,1)} custom-call(bf16[12,384,128]{2,1,0:T(8,128)(2,1)} %z_ref.1, s32[384]{0:T(512)} %mask_s.1, s32[1,384]{1,0:T(1,128)} %reshape.3.mask_v, f32[2,128]{1,0:T(2,128)} %ng_ref.1, bf16[2,128,512]{2,1,0:T(8,128)(2,1)} %ew_ref.1, bf16[2,128,128]{2,1,0:T(8,128)(2,1)} %gw_ref.1, bf16[2,128,128]{2,1,0:T(8,128)(2,1)} %ow_ref.1, ...), custom_call_target="tpu_custom_call" | custom-call | flops 2717908992 | bytes 2359296 | tf_op jit(solution)/shard_map/pallas_call | solution.py:312
  160.1 2.4 %copy.9 = bf16[12,384,128]{2,1,0:T(8,128)(2,1)} copy(bf16[12,384,128]{2,1,0:T(8,128)(2,1)} %shard_map.73) | data formatting | bytes 2359296

commit v3 on v2

--- a/solution.py
+++ b/solution.py
@@ -21,10 +21,11 @@
 
 def kernel(
     n, n_sub,
-    z_ref, mask_s, mask_v, ng_ref, ew_ref, gw_ref, ow_ref, mg_ref,
+    z_in, mask_s, mask_in, ng_in, ew_in, gw_in, ow_in, mg_in,
     out_ref,
-    wt, gain, normed, send_l, send_r, recv_l, recv_r, stage, lh, rh, mf, send_m, recv_m,
-    ss_l, ss_r, ss_m, rs_l, rs_r, rs_m,
+    z_ref, mask_v, ng_ref, ew_ref, gw_ref, ow_ref, mg_ref, in_sem,
+    wt, gain, normed, send_l, send_r, recv_l, recv_r, recv_n, stage, lh, rh, mf, send_m, recv_m,
+    ss_l, ss_r, ss_n, ss_m, rs_l, rs_r, rs_n, rs_m,
 ):
     rows, cols, _ = z_ref.shape
     hidden = ow_ref.shape[1]
@@ -53,6 +54,12 @@
     def lanes(v):
         return pl.ds(pl.multiple_of(v * LANES, LANES), LANES)
 
+    loads = [pltpu.make_async_copy(src, dst, in_sem.at[i]) for i, (src, dst) in enumerate((
+        (ew_in, ew_ref), (z_in, z_ref), (mask_in, mask_v), (ng_in, ng_ref), (gw_in, gw_ref),
+        (ow_in, ow_ref), (mg_in, mg_ref)))]
+    for load in loads:
+        load.start()
+
     barrier = pltpu.get_barrier_semaphore()
     loop(1, n, lambda k: pl.semaphore_signal(
         barrier, inc=1, device_id=device(lax.rem(me + k, n)),
@@ -70,6 +77,9 @@
         return remote(
             send_r.at[lax.rem(p, owners), v], recv_r.at[slot, v], ss_r.at[v, p], rs_r.at[v, slot], p)
 
+    def next_copy(v, q, slot):
+        return remote(send_r.at[q, v], recv_n.at[slot, v], ss_n.at[v, q], rs_n.at[v, slot], first + q)
+
     def mix_copy(v, q, p, slot):
         return remote(send_m.at[q, v], recv_m.at[slot, v], ss_m.at[v, p], rs_m.at[v, slot], p)
 
@@ -81,8 +91,8 @@
         loop(1, owners, lambda k: left_copy(v, lax.rem(mine + k, owners), mine).start())
 
     def start_right(v):
-        recv_r[me, v] = send_r[mine, v]
-        loop(1, owners, lambda k: right_copy(v, away(k, 0), me).start())
+        recv_n[mine, v] = send_r[mine, v]
+        loop(1, owners, lambda k: next_copy(v, lax.rem(mine + k, owners), mine).start())
 
     def start_all(v, last):
         recv_l[mine, v] = send_l[mine, v]
@@ -110,7 +120,7 @@
         nr = (centered * lax.rsqrt(var + 1e-05) * ng_ref[pl.ds(t, 1), :]).astype(BF16)
         normed[pl.ds(2 * u, 2), lanes(v), :] = nr.reshape(2, LANES, -1)
         proj = lax.dot_general(wt[...], nr, (((1,), (1,)), ((), ())), preferred_element_type=F32)
-        columns = mask_v[:, lanes(v)].astype(F32)
+        columns = mask_v[lanes(v)].astype(F32).reshape(1, LANES)
         mask = jnp.concatenate(
             [columns * mask_s[me * rows + 2 * u + i].astype(F32) for i in range(2)], axis=1)
         at = pl.ds(pl.multiple_of(u * TILE, TILE), TILE)
@@ -156,12 +166,19 @@
                 left_copy(v, q, q).wait_recv()
         loop(g * GROUP, (g + 1) * GROUP, one)
 
-    def wait_right(base, g, v):
+    def wait_right(g, v):
         def one(p):
             @pl.when(p != me)
             def _():
                 right_copy(v, p, p).wait_recv()
-        loop(base + g * GROUP, base + (g + 1) * GROUP, one)
+        loop(g * GROUP, (g + 1) * GROUP, one)
+
+    def wait_next(g, v):
+        def one(q):
+            @pl.when(q != mine)
+            def _():
+                next_copy(v, q, q).wait_recv()
+        loop(g * GROUP, (g + 1) * GROUP, one)
 
     def prepare(t):
         wt[...] = ew_ref[t].astype(F32).T.astype(BF16)
@@ -178,10 +195,15 @@
 
                 @pl.when(k > 0)
                 def _():
-                    right_copy(v, away(k, 0), me).wait_send()
+                    if t == 0:
+                        right_copy(v, away(k, 0), me).wait_send()
+                    else:
+                        next_copy(v, lax.rem(mine + k, owners), mine).wait_send()
                     left_copy(v, lax.rem(mine + k, owners), mine).wait_send()
         loop(0, owners, one)
 
+    for load in loads:
+        load.wait()
     prepare(0)
     prepare_gain(0)
     for v in range(chunks):
@@ -201,14 +223,12 @@
     def right_in(i):
         g = turn(i, n // GROUP)
         for v in range(chunks):
-            wait_right(0, g, v)
+            wait_right(g, v)
             sort(recv_r, 0, rh, g, v)
 
-    done, sorted_by = 0, None
+    done = 0
     for s in range(chunks):
         need = -(-(s + 1) * LANES // (GROUP * rows))
-        if sorted_by is None and need >= (splits + 1) // 2 * groups:
-            sorted_by = s
         loop(done, need, right_in)
         done = need
         v = turn(s, chunks)
@@ -236,8 +256,8 @@
         loop(1, owners, mix_in)
         loop(0, pairs, lambda u: project(1, u, v, finish(0, u, v, z_ref)))
         start_left(v)
-        if s == sorted_by:
-            start_right(turn(0, chunks))
+        if s == 0:
+            start_right(v)
     for s in range(1, chunks):
         start_right(turn(s, chunks))
     prepare_gain(1)
@@ -247,6 +267,17 @@
             mix_copy(v, lax.rem(mine + k, owners), away(k, 0), me).wait_send()
     loop(1, owners, mix_out)
 
+    def right_again(v):
+        def one(g):
+            wait_next(g, v)
+            sort(recv_n, 0, rh, g, v)
+        loop(0, groups, one)
+
+    def pack(p, v):
+        send_m[p, v] = mf[pl.ds(pl.multiple_of(p * block, TILE), block), :].astype(BF16)
+
+    start = turn(0, chunks)
+    done = 0
     for s in range(chunks):
         v = turn(s, chunks)
 
@@ -254,28 +285,39 @@
             wait_left(g, v)
             sort(recv_l, 0, lh, g, v)
         loop(0, groups, left_again)
-    for s in range(chunks):
+        if s == 0:
+            right_again(start)
+        for h in range(PER):
+            mf[pl.ds(v * (LANES * PER) + h, LANES, stride=PER), :] = lax.dot_general(
+                lh[h, :, lanes(v)], rh[h, pl.ds(0, part), lanes(start)], (((0,), (0,)), ((), ())),
+                preferred_element_type=F32)
+        ready = (s + 1) * LANES // rows
+
+        def hand_some(k, lo=done, count=ready - done):
+            p = turn(lo + lax.rem(mine + k, count), n)
+            pack(p, start)
+
+            @pl.when(p != me)
+            def _():
+                mix_copy(start, p, p, me).start()
+        loop(0, ready - done, hand_some)
+        done = ready
+    recv_m[me, start] = send_m[me, start]
+    for s in range(1, chunks):
         v = turn(s, chunks)
-
-        def right_again(g):
-            wait_right(first, g, v)
-            sort(recv_r, first, rh, g, v)
-        loop(0, groups, right_again)
+        right_again(v)
         for h in range(PER):
             mf[pl.ds(h, cols, stride=PER), :] = lax.dot_general(
                 lh[h], rh[h, pl.ds(0, part), lanes(v)], (((0,), (0,)), ((), ())),
                 preferred_element_type=F32)
 
-        def pack(p):
-            send_m[p, v] = mf[pl.ds(pl.multiple_of(p * block, TILE), block), :].astype(BF16)
-
         def hand_out(k):
             for i in range(1, splits):
                 p = away(k, i)
-                pack(p)
+                pack(p, v)
                 mix_copy(v, p, p, me).start()
             p = away(k, 0)
-            pack(p)
+            pack(p, v)
 
             @pl.when(k > 0)
             def _():
@@ -307,40 +349,46 @@
     block = rows * PER
     chunks = cols // LANES
     vmem = pl.BlockSpec(memory_space=pltpu.VMEM)
+    hbm = pl.BlockSpec(memory_space=pltpu.HBM)
     dma = pltpu.SemaphoreType.DMA
     flops = 2 * 2 * rows * cols * chan * (5 * hidden + chan) + 2 * 2 * PER * owners * rows * cols * cols
+    operands = (pair_state, residue_mask, norm_gain, edge_weight, gate_weight, out_weight, mix_gain)
+    scratch = [pltpu.VMEM(x.shape, x.dtype) for x in operands] + [dma((len(operands),))] + [
+        pltpu.VMEM((4 * hidden, chan), BF16),
+        pltpu.VMEM((hidden, 1), F32),
+        pltpu.VMEM((rows, cols, chan), BF16),
+        pltpu.VMEM((owners, chunks, block, LANES), BF16),
+        pltpu.VMEM((owners, chunks, block, LANES), BF16),
+        pltpu.VMEM((owners, chunks, block, LANES), BF16),
+        pltpu.VMEM((n, chunks, block, LANES), BF16),
+        pltpu.VMEM((owners, chunks, block, LANES), BF16),
+        pltpu.VMEM((GROUP * block, LANES), F32),
+        pltpu.VMEM((PER, owners * rows, cols), BF16),
+        pltpu.VMEM((PER, n * rows, cols), BF16),
+        pltpu.VMEM((PER * cols, LANES), F32),
+        pltpu.VMEM((n, chunks, block, LANES), BF16),
+        pltpu.VMEM((n, chunks, block, LANES), BF16),
+        dma((chunks, owners)),
+        dma((chunks, n)),
+        dma((chunks, owners)),
+        dma((chunks, n)),
+        dma((chunks, owners)),
+        dma((chunks, n)),
+        dma((chunks, owners)),
+        dma((chunks, n)),
+    ]
     return pl.pallas_call(
         functools.partial(kernel, n, n_sub),
         out_shape=jax.ShapeDtypeStruct(pair_state.shape, BF16),
-        in_specs=[vmem, pl.BlockSpec(memory_space=pltpu.SMEM)] + [vmem] * 6,
+        in_specs=[hbm, pl.BlockSpec(memory_space=pltpu.SMEM)] + [hbm] * 6,
         out_specs=vmem,
-        scratch_shapes=[
-            pltpu.VMEM((4 * hidden, chan), BF16),
-            pltpu.VMEM((hidden, 1), F32),
-            pltpu.VMEM((rows, cols, chan), BF16),
-            pltpu.VMEM((owners, chunks, block, LANES), BF16),
-            pltpu.VMEM((owners, chunks, block, LANES), BF16),
-            pltpu.VMEM((owners, chunks, block, LANES), BF16),
-            pltpu.VMEM((n, chunks, block, LANES), BF16),
-            pltpu.VMEM((GROUP * block, LANES), F32),
-            pltpu.VMEM((PER, owners * rows, cols), BF16),
-            pltpu.VMEM((PER, n * rows, cols), BF16),
-            pltpu.VMEM((PER * cols, LANES), F32),
-            pltpu.VMEM((n, chunks, block, LANES), BF16),
-            pltpu.VMEM((n, chunks, block, LANES), BF16),
-            dma((chunks, owners)),
-            dma((chunks, n)),
-            dma((chunks, n)),
-            dma((chunks, owners)),
-            dma((chunks, n)),
-            dma((chunks, n)),
-        ],
+        scratch_shapes=scratch,
         compiler_params=pltpu.CompilerParams(
             collective_id=0, has_side_effects=True, vmem_limit_bytes=60 * 2**20),
         cost_estimate=pl.CostEstimate(
             flops=flops, bytes_accessed=4 * rows * cols * chan, transcendentals=0),
     )(
-        pair_state, residue_mask, residue_mask.reshape(1, -1), norm_gain, edge_weight,
+        pair_state, residue_mask, residue_mask, norm_gain, edge_weight,
         gate_weight, out_weight, mix_gain,
     )
 

time: 163 us -> 162 us (level)
  no operation moved by 1% of the time
where the time goes in v3:
time: 162 us; the launch traced here: 161 us
  Pallas kernels  159 us (98%)
  local copies, waits for them, and re-layouts  2.36 us (1%)
    pallas_call x1, Pallas kernels, on_device(): pl.pallas_call(functools.partial(kernel, n, n_sub), out_shape=jax.ShapeDt...  159 us

profile of v3, /device:TPU:0, one launch (start us, length us, event | category | flops | bytes accessed | tf_op | source)
XLA Modules:
  0.0 161.5 jit_solution(17972787108677496156)
XLA Ops:
  0.0 159.1 %shard_map.73 = bf16[12,384,128]{2,1,0:T(8,128)(2,1)} custom-call(bf16[12,384,128]{2,1,0:T(8,128)(2,1)} %z_in.1, s32[384]{0:T(512)} %mask_in.1, s32[384]{0:T(512)} %mask_in.1, f32[2,128]{1,0:T(2,128)} %ng_in.1, bf16[2,128,512]{2,1,0:T(8,128)(2,1)} %ew_in.1, bf16[2,128,128]{2,1,0:T(8,128)(2,1)} %gw_in.1, bf16[2,128,128]{2,1,0:T(8,128)(2,1)} %ow_in.1, ...), custom_call_target="tpu_custom_call" | custom-call | flops 2717908992 | bytes 2359296 | tf_op jit(solution)/shard_map/pallas_call | solution.py:380
  159.1 2.4 %copy.9 = bf16[12,384,128]{2,1,0:T(8,128)(2,1)} copy(bf16[12,384,128]{2,1,0:T(8,128)(2,1)} %shard_map.73) | data formatting | bytes 2359296

commit v4 on v3

--- a/solution.py
+++ b/solution.py
@@ -21,9 +21,8 @@
 
 def kernel(
     n, n_sub,
-    z_in, mask_s, mask_in, ng_in, ew_in, gw_in, ow_in, mg_in,
+    z_ref, mask_s, mask_v, ng_ref, ew_ref, gw_ref, ow_ref, mg_ref,
     out_ref,
-    z_ref, mask_v, ng_ref, ew_ref, gw_ref, ow_ref, mg_ref, in_sem,
     wt, gain, normed, send_l, send_r, recv_l, recv_r, recv_n, stage, lh, rh, mf, send_m, recv_m,
     ss_l, ss_r, ss_n, ss_m, rs_l, rs_r, rs_n, rs_m,
 ):
@@ -54,12 +53,6 @@
     def lanes(v):
         return pl.ds(pl.multiple_of(v * LANES, LANES), LANES)
 
-    loads = [pltpu.make_async_copy(src, dst, in_sem.at[i]) for i, (src, dst) in enumerate((
-        (ew_in, ew_ref), (z_in, z_ref), (mask_in, mask_v), (ng_in, ng_ref), (gw_in, gw_ref),
-        (ow_in, ow_ref), (mg_in, mg_ref)))]
-    for load in loads:
-        load.start()
-
     barrier = pltpu.get_barrier_semaphore()
     loop(1, n, lambda k: pl.semaphore_signal(
         barrier, inc=1, device_id=device(lax.rem(me + k, n)),
@@ -103,10 +96,10 @@
                 right_copy(v, away(k, s), me).start()
 
         def near(k):
+            left_copy(v, lax.rem(mine + k, owners), mine).start()
+            right_copy(v, away(k, 0), me).start()
             if not last:
                 far(k)
-            right_copy(v, away(k, 0), me).start()
-            left_copy(v, lax.rem(mine + k, owners), mine).start()
         loop(1, owners, near)
         if last:
             loop(0, owners, far)
@@ -202,8 +195,6 @@
                     left_copy(v, lax.rem(mine + k, owners), mine).wait_send()
         loop(0, owners, one)
 
-    for load in loads:
-        load.wait()
     prepare(0)
     prepare_gain(0)
     for v in range(chunks):
@@ -349,40 +340,37 @@
     block = rows * PER
     chunks = cols // LANES
     vmem = pl.BlockSpec(memory_space=pltpu.VMEM)
-    hbm = pl.BlockSpec(memory_space=pltpu.HBM)
     dma = pltpu.SemaphoreType.DMA
     flops = 2 * 2 * rows * cols * chan * (5 * hidden + chan) + 2 * 2 * PER * owners * rows * cols * cols
-    operands = (pair_state, residue_mask, norm_gain, edge_weight, gate_weight, out_weight, mix_gain)
-    scratch = [pltpu.VMEM(x.shape, x.dtype) for x in operands] + [dma((len(operands),))] + [
-        pltpu.VMEM((4 * hidden, chan), BF16),
-        pltpu.VMEM((hidden, 1), F32),
-        pltpu.VMEM((rows, cols, chan), BF16),
-        pltpu.VMEM((owners, chunks, block, LANES), BF16),
-        pltpu.VMEM((owners, chunks, block, LANES), BF16),
-        pltpu.VMEM((owners, chunks, block, LANES), BF16),
-        pltpu.VMEM((n, chunks, block, LANES), BF16),
-        pltpu.VMEM((owners, chunks, block, LANES), BF16),
-        pltpu.VMEM((GROUP * block, LANES), F32),
-        pltpu.VMEM((PER, owners * rows, cols), BF16),
-        pltpu.VMEM((PER, n * rows, cols), BF16),
-        pltpu.VMEM((PER * cols, LANES), F32),
-        pltpu.VMEM((n, chunks, block, LANES), BF16),
-        pltpu.VMEM((n, chunks, block, LANES), BF16),
-        dma((chunks, owners)),
-        dma((chunks, n)),
-        dma((chunks, owners)),
-        dma((chunks, n)),
-        dma((chunks, owners)),
-        dma((chunks, n)),
-        dma((chunks, owners)),
-        dma((chunks, n)),
-    ]
     return pl.pallas_call(
         functools.partial(kernel, n, n_sub),
         out_shape=jax.ShapeDtypeStruct(pair_state.shape, BF16),
-        in_specs=[hbm, pl.BlockSpec(memory_space=pltpu.SMEM)] + [hbm] * 6,
+        in_specs=[vmem, pl.BlockSpec(memory_space=pltpu.SMEM)] + [vmem] * 6,
         out_specs=vmem,
-        scratch_shapes=scratch,
+        scratch_shapes=[
+            pltpu.VMEM((4 * hidden, chan), BF16),
+            pltpu.VMEM((hidden, 1), F32),
+            pltpu.VMEM((rows, cols, chan), BF16),
+            pltpu.VMEM((owners, chunks, block, LANES), BF16),
+            pltpu.VMEM((owners, chunks, block, LANES), BF16),
+            pltpu.VMEM((owners, chunks, block, LANES), BF16),
+            pltpu.VMEM((n, chunks, block, LANES), BF16),
+            pltpu.VMEM((owners, chunks, block, LANES), BF16),
+            pltpu.VMEM((GROUP * block, LANES), F32),
+            pltpu.VMEM((PER, owners * rows, cols), BF16),
+            pltpu.VMEM((PER, n * rows, cols), BF16),
+            pltpu.VMEM((PER * cols, LANES), F32),
+            pltpu.VMEM((n, chunks, block, LANES), BF16),
+            pltpu.VMEM((n, chunks, block, LANES), BF16),
+            dma((chunks, owners)),
+            dma((chunks, n)),
+            dma((chunks, owners)),
+            dma((chunks, n)),
+            dma((chunks, owners)),
+            dma((chunks, n)),
+            dma((chunks, owners)),
+            dma((chunks, n)),
+        ],
         compiler_params=pltpu.CompilerParams(
             collective_id=0, has_side_effects=True, vmem_limit_bytes=60 * 2**20),
         cost_estimate=pl.CostEstimate(

time: 162 us -> 159 us (0.981)
  Pallas kernels: 159 us -> 155 us
    pallas_call x1, Pallas kernels: 159 us -> 155 us  [on_device(): pl.pallas_call(functools.partial(kernel, n, n_sub), out_shape=jax.ShapeDt...]
where the time goes in v4:
time: 159 us; the launch traced here: 158 us
  Pallas kernels  155 us (97%)
  local copies, waits for them, and re-layouts  2.36 us (1%)
    pallas_call x1, Pallas kernels, on_device(): pl.pallas_call(functools.partial(kernel, n, n_sub), out_shape=jax.ShapeDt...  155 us

profile of v4, /device:TPU:0, one launch (start us, length us, event | category | flops | bytes accessed | tf_op | source)
XLA Modules:
  0.0 157.8 jit_solution(3354327119529552171)
XLA Ops:
  0.0 155.5 %shard_map.73 = bf16[12,384,128]{2,1,0:T(8,128)(2,1)} custom-call(bf16[12,384,128]{2,1,0:T(8,128)(2,1)} %z_ref.1, s32[384]{0:T(512)} %mask_v.1, s32[384]{0:T(512)} %mask_v.1, f32[2,128]{1,0:T(2,128)} %ng_ref.1, bf16[2,128,512]{2,1,0:T(8,128)(2,1)} %ew_ref.1, bf16[2,128,128]{2,1,0:T(8,128)(2,1)} %gw_ref.1, bf16[2,128,128]{2,1,0:T(8,128)(2,1)} %ow_ref.1, ...), custom_call_target="tpu_custom_call" | custom-call | flops 2717908992 | bytes 2359296 | tf_op jit(solution)/shard_map/pallas_call | solution.py:345
  155.5 2.4 %copy.9 = bf16[12,384,128]{2,1,0:T(8,128)(2,1)} copy(bf16[12,384,128]{2,1,0:T(8,128)(2,1)} %shard_map.73) | data formatting | bytes 2359296
